TPU v7x, 768 devices: a whole 4x8x12 slice. The times are simulated.
768 devices in a mesh: dp: 3 (over z_lo), mp: 64 (over z_hi, y, core), inner: 4 (over x).
Axes of the slice: x: 4, y: 8, z: 12 (z_hi: 4, z_lo: 3; z = z_hi * 3 + z_lo), core: 2. Of those that a mesh axis runs over, the one named last changes fastest.
Arguments:
- grads: bfloat16 [3, 3, 256, 512, 512], P('dp', None, None, 'mp', 'inner'), may hold values from -33 to 33, as said below
- table: int32 [3, 256, 1], P('dp'), may hold values from 0 to 63; in each aligned block of 256 rows (0 to 255, 256 to 511, ..., all dimensions but the last counted through in order) at most 8 rows name the same one
- left_root: bfloat16 [3, 64, 8, 512, 512], P('dp', 'mp'), may hold values from -1 to 9, as said below
- right_root: bfloat16 [3, 64, 8, 512, 512], P('dp', 'mp', None, None, 'inner'), may hold values from -1 to 9, as said below
Outputs:
- directions: bfloat16 [3, 256, 512, 512], P('dp', None, 'mp', 'inner')
Inputs may be any that keep to these rules, and one draw needn't show every extreme that they name: `table`: in each span no owner holds more than 8 blocks, and in some span one owner holds exactly 8. `grads`: each replica's gradient block. `left_root`: slot c of owner o in span d holds the factor of the c-th block of span d that the table gives to o; slots beyond an owner's count are not read. `right_root`: laid out in slots as left_root.
All inputs are finite; a program needn't handle non-finite values.
Results may differ from a plain program's by a relative error of at most 0.014.
Values may be sent and summed in bfloat16 or wider, within the bound.
No kernel may reach another device: no remote copies, remote signals or barrier semaphores. Data moves between devices by JAX's collectives and lax.ppermute only.
A program may use at most 32 MiB of HBM per device.

v0:
```python
import jax
import jax.numpy as jnp
from jax import lax
from jax.sharding import PartitionSpec as P


def shards(grads, table, left_root, right_root):
    owners_count = lax.axis_size("mp")
    capacity = left_root.shape[2]
    group_len = grads.shape[2]
    summed = lax.psum_scatter(grads[0], "dp", scatter_dimension=0, tiled=True).astype(jnp.float32)
    gradient = summed[0].astype(jnp.bfloat16)
    row_len = gradient.shape[1]
    col_len = gradient.shape[2]
    owner = table[0, :, 0]
    onehot = (owner[:, None] == jnp.arange(owners_count, dtype=jnp.int32)[None, :]).astype(
        jnp.int32
    )
    rank = jnp.sum((jnp.cumsum(onehot, axis=0) - onehot) * onehot, axis=1)
    target = owner * capacity + rank
    slot_total = owners_count * capacity
    pick_send = (target[None, :] == jnp.arange(slot_total, dtype=jnp.int32)[:, None]).astype(
        jnp.bfloat16
    )
    outgoing = jnp.dot(
        pick_send,
        gradient.reshape(group_len, row_len * col_len),
        preferred_element_type=jnp.float32,
    )
    outgoing = outgoing.astype(jnp.bfloat16).reshape(owners_count, capacity, row_len, col_len)
    received = lax.all_to_all(outgoing, "mp", split_axis=0, concat_axis=2, tiled=True)
    owned = received[0]
    left = left_root[0, 0]
    right = right_root[0, 0]
    left_full = jnp.einsum(
        "cij,cjk->cik",
        left,
        lax.all_gather(owned, "inner", axis=2, tiled=True),
        preferred_element_type=jnp.float32,
    ).astype(jnp.bfloat16)
    product = jnp.einsum("cij,cjk->cik", left_full, right, preferred_element_type=jnp.float32)
    grad_part = jnp.sum(jnp.square(owned.astype(jnp.float32)), axis=(1, 2))
    pre_part = jnp.sum(jnp.square(product), axis=(1, 2))
    grad_square, pre_square = lax.psum((grad_part, pre_part), "inner")
    factor = jnp.sqrt(grad_square / (pre_square + 1e-06))
    direction = (product * factor[:, None, None]).astype(jnp.bfloat16)
    returned = lax.all_to_all(direction, "mp", split_axis=1, concat_axis=0, tiled=True)
    pick_back = (target[:, None] == jnp.arange(slot_total, dtype=jnp.int32)[None, :]).astype(
        jnp.bfloat16
    )
    gathered = jnp.dot(
        pick_back,
        returned.reshape(slot_total, row_len * col_len),
        preferred_element_type=jnp.float32,
    )
    return gathered.astype(jnp.bfloat16).reshape(1, group_len, row_len, col_len)


def solution(mesh):
    placed = (
        P("dp", None, None, "mp", "inner"),
        P("dp", None, None),
        P("dp", "mp", None, None, None),
        P("dp", "mp", None, None, "inner"),
    )
    return jax.shard_map(
        shards, mesh=mesh, in_specs=placed, out_specs=P("dp", None, "mp", "inner"), check_vma=False
    )
```

profile of v0, /device:TPU:1, one launch (start us, length us, event | category | flops | bytes accessed | tf_op | source)
XLA Modules:
  0.0 252.3 jit_solution(6379454113061673129)
XLA Ops:
  6.5 0.0 copy-start
  6.5 0.0 reduce-scatter.2.cloned.1.call-start
  6.5 0.7 reduce-scatter.2.cloned.1.call-update
  7.3 0.0 all-gather.2.cloned.1.call-start
  7.3 0.7 fusion.20
  8.0 0.6 reduce-window.6
  8.6 0.2 slice_reduce_fusion
  8.8 0.8 fusion.19
  9.6 0.7 multiply_add_fusion
  10.3 50.1 %reduce-scatter.2.cloned.1.call-done = bf16[1,256,8,128]{3,2,1,0:T(8,128)(2,1)} async-done(((bf16[3,256,8,128]{3,2,1,0:T(8,128)(2,1)}), bf16[1,256,8,128]{3,2,1,0:T(8,128)(2,1)}) %reduce-scatter.2.cloned.1.call-update) | async-done | bytes 524304 | tf_op jit(solution)/shard_map/reduce_scatter | solution.py:11
  60.4 1.5 fusion.8
  61.9 0.3 copy.19
  62.2 55.9 %all_to_all.30 = bf16[64,8,8,128]{3,2,1,0:T(8,128)(2,1)S(1)} all-to-all(bf16[64,8,8,128]{3,2,1,0:T(8,128)(2,1)S(1)} %copy.19), channel_id=1, replica_groups=mesh['dp'=3,'mp'=64,'inner'=4] {'mp'}, dimensions={0} | all-to-all | bytes 2097152 | tf_op jit(solution)/shard_map/all_to_all | solution.py:31
  118.0 0.2 copy.43
  118.2 1.3 copy.21
  119.6 0.0 all-gather.2.cloned.1.call-update
  119.6 0.2 multiply_reduce_fusion.1
  119.8 53.5 %all-gather.2.cloned.1.call-done = bf16[8,512,512]{1,2,0:T(8,128)(2,1)} async-done(((bf16[8,512,128]{1,2,0:T(8,128)(2,1)}), bf16[8,512,512]{1,2,0:T(8,128)(2,1)}) %all-gather.2.cloned.1.call-update) | async-done | bytes 4194320 | tf_op jit(solution)/shard_map/all_gather | solution.py:38
  173.2 0.0 copy-done
  173.2 6.1 %multiply_reduce_fusion = (f32[8]{0:T(128)S(1)}, f32[8,512,128]{2,1,0:T(8,128)S(1)}) fusion(bf16[1,1,8,512,128]{4,3,2,1,0:T(8,128)(2,1)S(1)} %copy-done, bf16[8,512,512]{1,2,0:T(8,128)(2,1)} %all-gather.2.cloned.1.call-done, bf16[1,1,8,512,512]{4,3,2,1,0:T(8,128)(2,1)} %param.6), kind=kOutput, calls=%fused_computation.5 | convolution fusion | flops 2687500288 | bytes 11534368 | tf_op jit(solution)/shard_map/cij,cjk->cik/dot_general | solution.py:41
  179.3 6.6 %all-reduce = (f32[8]{0:T(128)S(1)}, f32[8]{0:T(128)S(1)}) all-reduce(f32[8]{0:T(128)S(1)} %multiply_reduce_fusion.1, f32[8]{0:T(128)S(1)} %get-tuple-element.7), channel_id=1, replica_groups=mesh['dp'=3,'mp'=64,'inner'=4] {'inner'}, use_global_device_ids=true, to_apply=%region_5.6 | all-reduce | flops 16 | bytes 128 | tf_op jit(solution)/shard_map/psum | solution.py:44
  185.9 0.3 multiply_convert_fusion
  186.2 0.7 copy.23
  186.9 56.9 %all_to_all.31 = bf16[8,512,128]{2,0,1:T(8,128)(2,1)S(1)} all-to-all(bf16[8,512,128]{2,0,1:T(8,128)(2,1)S(1)} %copy.23), channel_id=1, replica_groups=mesh['dp'=3,'mp'=64,'inner'=4] {'mp'}, dimensions={1} | all-to-all | bytes 2097152 | tf_op jit(solution)/shard_map/all_to_all | solution.py:47
  243.7 0.3 copy.42
  244.0 0.5 fusion.9
  244.5 0.9 copy.29
  (3 shorter events, 0.1 us)
Async XLA Ops:
  6.5 166.7 %copy-start = (bf16[1,1,8,512,128]{4,3,2,1,0:T(8,128)(2,1)S(1)}, bf16[1,1,8,512,128]{4,3,2,1,0:T(8,128)(2,1)}, u32[]{:S(2)}) copy-start(bf16[1,1,8,512,128]{4,3,2,1,0:T(8,128)(2,1)} %param.7) | copy-start | bytes 3145732
  6.5 53.9 %reduce-scatter.2.cloned.1.call-start = ((), (), s32[]{:S(2)}) async-start(), calls=%async_computation.3 | async-start | bytes 2097152 | tf_op jit(solution)/shard_map/reduce_scatter | solution.py:11
  7.3 166.0 %all-gather.2.cloned.1.call-start = ((), (), s32[]{:S(2)}) async-start(), calls=%async_computation.4 | async-start | bytes 5242880 | tf_op jit(solution)/shard_map/all_gather | solution.py:38
Sparse Core Ops, SparseCore 0:
  10.5 49.8 reduce-scatter.1
  119.7 53.4 all-gather.1
where the time goes:
time: 254 us; the launch traced here: 252 us
  blocking collectives  119 us (47%)
  waiting for transfers between devices  104 us (41%)
  between operations  13.5 us (5%)
  matrix products  8.05 us (3%)
  local copies, waits for them, and re-layouts  3.83 us (2%)
  other arithmetic  3.25 us (1%)
    all_to_all x1, blocking collectives, shards(): lax.all_to_all(direction, 'mp', split_axis=1, concat_axis=0, tiled=True)  56.9 us
    all_to_all x1, blocking collectives, shards(): lax.all_to_all(outgoing, 'mp', split_axis=0, concat_axis=2, tiled=True)  55.9 us
    all_gather x1, waiting for transfers between devices, shards(): lax.all_gather(owned, 'inner', axis=2, tiled=True)  53.5 us
    reduce_scatter x1, waiting for transfers between devices, shards(): lax.psum_scatter(grads[0], 'dp', scatter_dimension=0, tiled=True)  50.1 us
    psum x1, blocking collectives, shards(): grad_square, pre_square = lax.psum((grad_part, pre_part), 'inner')  6.59 us
    dot_general x1, matrix products, shards(): jnp.einsum('cij,cjk->cik', left_full, right, preferred_element_type=jnp.f...  6.08 us
  transfers between devices with their start and end apart: 2, of which 2 were waited for; matrix products, arithmetic and copies ran while one was open for 1% of the time, Pallas kernels for 0%

commit v1 on v0

v1 whole, which is shorter than its diff:
```python
import functools

import jax
import jax.numpy as jnp
from jax import lax
from jax.experimental import pallas as pl
from jax.experimental.pallas import tpu as pltpu
from jax.sharding import PartitionSpec as P

GROUP_AXES = ("mp", "inner")


def ring(size, step):
    return [(i, (i + step) % size) for i in range(size)]


def grafted(received_ref, left_ref, right_ref, out_ref):
    pieces, parts, pair_rows, lanes = received_ref.shape
    held = left_ref.shape[0]
    row_len = pair_rows // held
    directions = []
    for slot in range(held):
        rows = slice(slot * row_len, (slot + 1) * row_len)
        gradient = jnp.concatenate(
            [
                received_ref[:, part]
                .astype(jnp.float32)[:, rows]
                .reshape(pieces * row_len, lanes)
                for part in range(parts)
            ],
            axis=1,
        )
        left = jnp.dot(
            left_ref[slot], gradient.astype(jnp.bfloat16), preferred_element_type=jnp.float32
        ).astype(jnp.bfloat16)
        right = jnp.concatenate([right_ref[part, slot] for part in range(parts)], axis=1)
        product = jnp.dot(left, right, preferred_element_type=jnp.float32)
        grad_square = jnp.sum(jnp.square(gradient))
        pre_square = jnp.sum(jnp.square(product))
        factor = jnp.sqrt(jnp.full((1, lanes), grad_square / (pre_square + 1e-06), jnp.float32))
        directions.append(product * factor[:, :1])
    for part in range(parts):
        columns = slice(part * lanes, (part + 1) * lanes)
        out_ref[:, part] = jnp.concatenate(
            [each[:, columns].reshape(pieces, row_len, lanes) for each in directions], axis=1
        ).astype(jnp.bfloat16)


def shards(grads, table, left_root, right_root):
    replicas = lax.axis_size("dp")
    owners_count = lax.axis_size("mp")
    parts = lax.axis_size("inner")
    capacity = left_root.shape[2]
    held = capacity // parts
    _, _, group_len, row_len, col_len = grads.shape
    slot_total = owners_count * capacity
    me = lax.axis_index("dp")
    inner = lax.axis_index("inner")

    terms = [lax.dynamic_index_in_dim(grads[0], me, 0, keepdims=False)]
    for step in range(1, replicas):
        other = lax.rem(me + step, replicas)
        sent = lax.dynamic_index_in_dim(grads[0], other, 0, keepdims=False)
        terms.append(lax.ppermute(sent, "dp", ring(replicas, step)))

    right = lax.all_to_all(
        right_root[0, 0].reshape(parts, held, *right_root.shape[3:]), "inner", 0, 0, tiled=True
    )
    left = lax.dynamic_slice_in_dim(left_root[0, 0], inner * held, held, 0)

    owner = table[0, :, 0]
    onehot = (owner[:, None] == jnp.arange(owners_count, dtype=jnp.int32)[None, :]).astype(
        jnp.int32
    )
    rank = jnp.sum((jnp.cumsum(onehot, axis=0) - onehot) * onehot, axis=1)
    target = owner * capacity + rank
    slots = jnp.arange(slot_total, dtype=jnp.int32)
    pick_send = (target[None, :] == slots[:, None]).astype(jnp.bfloat16)
    pick_back = (target[:, None] == slots[None, :]).astype(jnp.bfloat16)

    summed = functools.reduce(jnp.add, [term.astype(jnp.float32) for term in terms])
    gradient = summed.astype(jnp.bfloat16)
    outgoing = jnp.dot(
        pick_send,
        gradient.reshape(group_len, row_len * col_len),
        preferred_element_type=jnp.float32,
    ).astype(jnp.bfloat16)
    outgoing = outgoing.reshape(owners_count * parts, held * row_len, col_len)
    received = lax.all_to_all(outgoing, GROUP_AXES, 0, 0, tiled=True)
    received = received.reshape(owners_count, parts, held * row_len, col_len)
    direction = pl.pallas_call(
        grafted,
        out_shape=jax.ShapeDtypeStruct(received.shape, jnp.bfloat16),
        compiler_params=pltpu.CompilerParams(vmem_limit_bytes=40 * 1024 * 1024),
    )(received, left, right)
    returned = lax.all_to_all(
        direction.reshape(owners_count * parts, held * row_len, col_len),
        GROUP_AXES,
        0,
        0,
        tiled=True,
    )
    gathered = jnp.dot(
        pick_back,
        returned.reshape(slot_total, row_len * col_len),
        preferred_element_type=jnp.float32,
    )
    return gathered.astype(jnp.bfloat16).reshape(1, group_len, row_len, col_len)


def solution(mesh):
    placed = (
        P("dp", None, None, "mp", "inner"),
        P("dp", None, None),
        P("dp", "mp", None, None, None),
        P("dp", "mp", None, None, "inner"),
    )
    return jax.shard_map(
        shards, mesh=mesh, in_specs=placed, out_specs=P("dp", None, "mp", "inner"), check_vma=False
    )
```

time: 254 us -> 168 us (0.66)
  blocking collectives: 119 us -> 54.4 us
  waiting for transfers between devices: 104 us -> 61.9 us
  starting transfers between devices: 0.04 us -> 41.2 us
  between operations: 13.5 us -> 0.09 us
  matrix products: 8.05 us -> 0.94 us
    all_to_all x2 -> x1, blocking collectives: 113 us -> 54.4 us  [shards(): lax.all_to_all(direction.reshape(owners_count * parts, held * row_len, co...]
    all_gather x1 -> x0, waiting for transfers between devices: 53.5 us -> none  [shards(): lax.all_gather(owned, 'inner', axis=2, tiled=True)]
    reduce_scatter x1 -> x0, waiting for transfers between devices: 50.1 us -> none  [shards(): lax.psum_scatter(grads[0], 'dp', scatter_dimension=0, tiled=True)]
    all_to_all x0 -> x2, waiting for transfers between devices: none -> 44 us  [the longest x1 44 us: shards(): received = lax.all_to_all(outgoing, GROUP_AXES, 0, 0, tiled=True)]
    all_to_all x0 -> x2, starting transfers between devices: none -> 33.5 us  [the longest x1 28.5 us: shards(): received = lax.all_to_all(outgoing, GROUP_AXES, 0, 0, tiled=True)]
    ppermute x0 -> x2, waiting for transfers between devices: none -> 17.9 us  [shards(): terms.append(lax.ppermute(sent, 'dp', ring(replicas, step)))]
    ppermute x0 -> x2, starting transfers between devices: none -> 7.72 us  [shards(): terms.append(lax.ppermute(sent, 'dp', ring(replicas, step)))]
    psum x1 -> x0, blocking collectives: 6.59 us -> none  [shards(): grad_square, pre_square = lax.psum((grad_part, pre_part), 'inner')]
  transfers between devices with their start and end apart: 2 -> 4, of which waited for: 2 -> 3; matrix products, arithmetic and copies ran while one was open for 1% -> 4% of each run, Pallas kernels for 0% -> 0%
where the time goes in v1:
time: 168 us
  waiting for transfers between devices  61.9 us (37%)
  blocking collectives  54.4 us (32%)
  starting transfers between devices  41.2 us (25%)
  local copies, waits for them, and re-layouts  5.18 us (3%)
  other arithmetic  2.02 us (1%)
  Pallas kernels  1.83 us (1%)
    all_to_all x1, blocking collectives, shards(): lax.all_to_all(direction.reshape(owners_count * parts, held * row_len, co...  54.4 us
    all_to_all x1, waiting for transfers between devices, shards(): received = lax.all_to_all(outgoing, GROUP_AXES, 0, 0, tiled=True)  44 us
    all_to_all x1, starting transfers between devices, shards(): received = lax.all_to_all(outgoing, GROUP_AXES, 0, 0, tiled=True)  28.5 us
    ppermute x2, waiting for transfers between devices, shards(): terms.append(lax.ppermute(sent, 'dp', ring(replicas, step)))  17.9 us
    ppermute x2, starting transfers between devices, shards(): terms.append(lax.ppermute(sent, 'dp', ring(replicas, step)))  7.72 us
    all_to_all x1, starting transfers between devices, shards(): lax.all_to_all(right_root[0, 0].reshape(parts, held, *right_root.shape[3:...  4.97 us
  transfers between devices with their start and end apart: 4, of which 3 were waited for; matrix products, arithmetic and copies ran while one was open for 4% of the time, Pallas kernels for 0%

profile of v1, /device:TPU:1, one launch (start us, length us, event | category | flops | bytes accessed | tf_op | source)
XLA Modules:
  0.0 167.6 jit_solution(15599484637525801997)
XLA Ops:
  0.0 0.0 copy-start
  0.0 0.0 copy-start.1
  0.0 5.0 %all-to-all-start.1 = ((bf16[4,2,512,128]{3,2,1,0:T(8,128)(2,1)}), bf16[4,2,512,128]{3,2,1,0:T(8,128)(2,1)S(1)}, u32[]{:S(2)}, u32[]{:S(2)}) async-start(bf16[4,2,512,128]{3,2,1,0:T(8,128)(2,1)} %bitcast.45), calls=%async_computation.1 | async-start | bytes 2097152 | tf_op jit(solution)/shard_map/all_to_all | solution.py:66
  5.0 0.0 copy-done
  5.0 1.0 dynamic-slice_bitcast_fusion.2
  6.0 4.0 %collective-permute-start = (bf16[256,8,128]{2,1,0:T(8,128)(2,1)}, bf16[256,8,128]{2,1,0:T(8,128)(2,1)S(1)}, u32[]{:S(2)}, u32[]{:S(2)}) collective-permute-start(bf16[256,8,128]{2,1,0:T(8,128)(2,1)} %get-tuple-element.5), channel_id=1, source_target_pairs={{0,256},{256,512},{512,0},{1,257},{257,513},{513,1},{2,258},{258,5... | collective-permute-start | bytes 1572872 | tf_op jit(solution)/shard_map/ppermute | solution.py:64
  10.0 3.7 %collective-permute-start.1 = (bf16[256,8,128]{2,1,0:T(8,128)(2,1)}, bf16[256,8,128]{2,1,0:T(8,128)(2,1)}, u32[]{:S(2)}, u32[]{:S(2)}) collective-permute-start(bf16[256,8,128]{2,1,0:T(8,128)(2,1)} %get-tuple-element.6), channel_id=1, source_target_pairs={{0,512},{256,0},{512,256},{1,513},{257,1},{513,257},{2,514},{258,2... | collective-permute-start | bytes 1572872 | tf_op jit(solution)/shard_map/ppermute | solution.py:64
  13.7 0.0 copy-done.1
  13.8 0.6 reduce-window.6
  14.4 0.2 slice_reduce_fusion
  14.6 0.1 fusion.9
  14.7 4.2 %collective-permute-done = bf16[256,8,128]{2,1,0:T(8,128)(2,1)S(1)} collective-permute-done((bf16[256,8,128]{2,1,0:T(8,128)(2,1)}, bf16[256,8,128]{2,1,0:T(8,128)(2,1)S(1)}, u32[]{:S(2)}, u32[]{:S(2)}) %collective-permute-start) | collective-permute-done | bytes 524320 | tf_op jit(solution)/shard_map/ppermute | solution.py:64
  18.9 13.8 %collective-permute-done.1 = bf16[256,8,128]{2,1,0:T(8,128)(2,1)} collective-permute-done((bf16[256,8,128]{2,1,0:T(8,128)(2,1)}, bf16[256,8,128]{2,1,0:T(8,128)(2,1)}, u32[]{:S(2)}, u32[]{:S(2)}) %collective-permute-start.1) | collective-permute-done | bytes 524320 | tf_op jit(solution)/shard_map/ppermute | solution.py:64
  32.7 1.2 fusion.2
  33.9 0.5 convolution_convert_fusion
  34.4 1.3 reshape.62
  35.7 0.0 all-to-all-done.1.right_ref
  35.7 28.5 %all-to-all-start = ((bf16[256,16,128]{2,1,0:T(8,128)(2,1)}), bf16[256,16,128]{2,1,0:T(8,128)(2,1)S(1)}, u32[]{:S(2)}, u32[]{:S(2)}) async-start(bf16[256,16,128]{2,1,0:T(8,128)(2,1)} %reshape.62), calls=%async_computation | async-start | bytes 2097152 | tf_op jit(solution)/shard_map/all_to_all | solution.py:89
  64.2 1.3 dynamic-slice_bitcast_fusion.left_ref
  65.5 44.0 %all-to-all-done = bf16[256,16,128]{2,1,0:T(8,128)(2,1)S(1)} async-done(((bf16[256,16,128]{2,1,0:T(8,128)(2,1)}), bf16[256,16,128]{2,1,0:T(8,128)(2,1)S(1)}, u32[]{:S(2)}, u32[]{:S(2)}) %all-to-all-start) | async-done | bytes 1048608 | tf_op jit(solution)/shard_map/all_to_all | solution.py:89
  109.5 1.8 %shard_map.46 = bf16[64,4,16,128]{3,2,1,0:T(8,128)(2,1)S(1)} custom-call(bf16[64,4,16,128]{3,2,1,0:T(8,128)(2,1)S(1)} %bitcast.42, bf16[2,512,512]{2,1,0:T(8,128)(2,1)S(1)} %dynamic-slice_bitcast_fusion.left_ref, bf16[4,2,512,128]{3,2,1,0:T(8,128)(2,1)S(1)} %all-to-all-done.1.right_ref), custom_call_target="tpu_custom_call" | custom-call | tf_op jit(solution)/shard_map/pallas_call | solution.py:91
  111.3 54.4 %all_to_all.15 = bf16[256,16,128]{2,1,0:T(8,128)(2,1)S(1)} all-to-all(bf16[256,16,128]{2,1,0:T(8,128)(2,1)S(1)} %bitcast.43), channel_id=1, replica_groups=mesh['dp'=3,'mp'=64,'inner'=4] {'mp','inner'}, dimensions={0} | all-to-all | bytes 2097152 | tf_op jit(solution)/shard_map/all_to_all | solution.py:96
  165.7 0.5 reshape.65
  166.2 0.5 fusion
  166.7 0.9 copy.8
  (4 shorter events, 0.1 us)
Async XLA Ops:
  0.0 5.0 %copy-start = (bf16[1,3,256,8,128]{4,3,2,1,0:T(8,128)(2,1)S(1)}, bf16[1,3,256,8,128]{4,3,2,1,0:T(8,128)(2,1)}, u32[]{:S(2)}) copy-start(bf16[1,3,256,8,128]{4,3,2,1,0:T(8,128)(2,1)} %param.4) | copy-start | bytes 4718596
  0.0 13.7 %copy-start.1 = (s32[1,256,1]{1,2,0:T(1,128)S(1)}, s32[1,256,1]{1,2,0:T(1,128)}, u32[]{:S(2)}) copy-start(s32[1,256,1]{1,2,0:T(1,128)} %param.5) | copy-start | bytes 3076
  0.0 35.7 %all-to-all-start.1 = ((bf16[4,2,512,128]{3,2,1,0:T(8,128)(2,1)}), bf16[4,2,512,128]{3,2,1,0:T(8,128)(2,1)S(1)}, u32[]{:S(2)}, u32[]{:S(2)}) async-start(bf16[4,2,512,128]{3,2,1,0:T(8,128)(2,1)} %bitcast.45), calls=%async_computation.1 | async-start | bytes 2097152 | tf_op jit(solution)/shard_map/all_to_all | solution.py:66
  6.0 12.9 %collective-permute-start = (bf16[256,8,128]{2,1,0:T(8,128)(2,1)}, bf16[256,8,128]{2,1,0:T(8,128)(2,1)S(1)}, u32[]{:S(2)}, u32[]{:S(2)}) collective-permute-start(bf16[256,8,128]{2,1,0:T(8,128)(2,1)} %get-tuple-element.5), channel_id=1, source_target_pairs={{0,256},{256,512},{512,0},{1,257},{257,513},{513,1},{2,258},{258,5... | collective-permute-start | bytes 1572872 | tf_op jit(solution)/shard_map/ppermute | solution.py:64
  10.0 22.7 %collective-permute-start.1 = (bf16[256,8,128]{2,1,0:T(8,128)(2,1)}, bf16[256,8,128]{2,1,0:T(8,128)(2,1)}, u32[]{:S(2)}, u32[]{:S(2)}) collective-permute-start(bf16[256,8,128]{2,1,0:T(8,128)(2,1)} %get-tuple-element.6), channel_id=1, source_target_pairs={{0,512},{256,0},{512,256},{1,513},{257,1},{513,257},{2,514},{258,2... | collective-permute-start | bytes 1572872 | tf_op jit(solution)/shard_map/ppermute | solution.py:64
  35.7 73.8 %all-to-all-start = ((bf16[256,16,128]{2,1,0:T(8,128)(2,1)}), bf16[256,16,128]{2,1,0:T(8,128)(2,1)S(1)}, u32[]{:S(2)}, u32[]{:S(2)}) async-start(bf16[256,16,128]{2,1,0:T(8,128)(2,1)} %reshape.62), calls=%async_computation | async-start | bytes 2097152 | tf_op jit(solution)/shard_map/all_to_all | solution.py:89

commit v2 on v1

v2 whole, which is shorter than its diff:
```python
import jax
import jax.numpy as jnp
from jax import lax
from jax.experimental import pallas as pl
from jax.experimental.pallas import tpu as pltpu
from jax.sharding import PartitionSpec as P

GROUP_AXES = ("mp", "inner")
UNROLL = 8
VMEM_BYTES = 40 * 1024 * 1024


def ring(size, step):
    return [(i, (i + step) % size) for i in range(size)]


def whole(shape):
    return pl.BlockSpec(shape, lambda *_: (0,) * len(shape))


def picked(source_ref, span_ref, own_ref, *rest):
    *terms, out_ref, total = rest
    summed = own_ref[0].astype(jnp.float32)
    for term in terms:
        summed = summed + term[...].astype(jnp.float32)
    total[...] = summed.astype(jnp.bfloat16)
    copied(source_ref, total, out_ref)


def copied(place_ref, from_ref, to_ref):
    def step(turn, carry):
        for offset in range(UNROLL):
            at = turn * UNROLL + offset
            to_ref[at] = from_ref[place_ref[at]]
        return carry

    lax.fori_loop(0, to_ref.shape[0] // UNROLL, step, 0)


def grafted(received_ref, left_ref, right_ref, out_ref):
    pieces, parts, held, row_len, lanes = received_ref.shape
    for slot in range(held):
        gradient = jnp.concatenate(
            [
                received_ref[:, part, slot]
                .astype(jnp.float32)
                .reshape(pieces * row_len, lanes)
                for part in range(parts)
            ],
            axis=1,
        )
        left = jnp.dot(
            left_ref[slot], gradient.astype(jnp.bfloat16), preferred_element_type=jnp.float32
        ).astype(jnp.bfloat16)
        right = jnp.concatenate([right_ref[part, slot] for part in range(parts)], axis=1)
        product = jnp.dot(left, right, preferred_element_type=jnp.float32)
        grad_square = jnp.sum(jnp.square(gradient))
        pre_square = jnp.sum(jnp.square(product))
        factor = jnp.sqrt(jnp.full((1, lanes), grad_square / (pre_square + 1e-06), jnp.float32))
        direction = product * factor[:, :1]
        for part in range(parts):
            out_ref[:, part, slot] = (
                direction[:, part * lanes : (part + 1) * lanes]
                .reshape(pieces, row_len, lanes)
                .astype(jnp.bfloat16)
            )


def shards(grads, table, left_root, right_root):
    replicas = lax.axis_size("dp")
    owners_count = lax.axis_size("mp")
    parts = lax.axis_size("inner")
    capacity = left_root.shape[2]
    held = capacity // parts
    _, _, group_len, row_len, col_len = grads.shape
    slot_total = owners_count * capacity
    me = lax.axis_index("dp")
    inner = lax.axis_index("inner")
    params = pltpu.CompilerParams(vmem_limit_bytes=VMEM_BYTES)

    terms = []
    for step in range(1, replicas):
        other = lax.rem(me + step, replicas)
        sent = lax.dynamic_index_in_dim(grads[0], other, 0, keepdims=False)
        terms.append(lax.ppermute(sent, "dp", ring(replicas, step)))

    owner = table[0, :, 0]
    onehot = (owner[:, None] == jnp.arange(owners_count, dtype=jnp.int32)[None, :]).astype(
        jnp.int32
    )
    rank = jnp.sum((jnp.cumsum(onehot, axis=0) - onehot) * onehot, axis=1)
    target = owner * capacity + rank
    slots = jnp.arange(slot_total, dtype=jnp.int32)
    blocks = jnp.arange(group_len, dtype=jnp.int32)
    source = jnp.sum(
        jnp.where(target[None, :] == slots[:, None], blocks[None, :], 0), axis=1
    ).astype(jnp.int32)

    right = lax.all_to_all(
        right_root[0, 0].reshape(parts, held, *right_root.shape[3:]), "inner", 0, 0, tiled=True
    )
    left = lax.dynamic_slice_in_dim(left_root[0, 0], inner * held, held, 0)
    source, left, right = lax.optimization_barrier((source, left, right))

    piece = (group_len, row_len, col_len)
    sending = (slot_total, row_len, col_len)
    outgoing = pl.pallas_call(
        picked,
        grid_spec=pltpu.PrefetchScalarGridSpec(
            num_scalar_prefetch=2,
            grid=(1,),
            in_specs=[pl.BlockSpec((1, *piece), lambda _, source, span: (span[0], 0, 0, 0))]
            + [whole(piece)] * (replicas - 1),
            out_specs=whole(sending),
            scratch_shapes=[pltpu.VMEM(piece, jnp.bfloat16)],
        ),
        out_shape=jax.ShapeDtypeStruct(sending, jnp.bfloat16),
        compiler_params=params,
    )(source, jnp.full((1,), me, jnp.int32), grads[0], *terms)
    outgoing, left, right = lax.optimization_barrier((outgoing, left, right))
    received = lax.all_to_all(outgoing, GROUP_AXES, 0, 0, tiled=True)
    shape = (owners_count, parts, held, row_len, col_len)
    direction = pl.pallas_call(
        grafted,
        out_shape=jax.ShapeDtypeStruct(shape, jnp.bfloat16),
        compiler_params=params,
    )(received.reshape(shape), left, right)
    returned = lax.all_to_all(direction.reshape(sending), GROUP_AXES, 0, 0, tiled=True)
    result = pl.pallas_call(
        copied,
        grid_spec=pltpu.PrefetchScalarGridSpec(
            num_scalar_prefetch=1,
            grid=(1,),
            in_specs=[whole(sending)],
            out_specs=whole(piece),
        ),
        out_shape=jax.ShapeDtypeStruct(piece, jnp.bfloat16),
        compiler_params=params,
    )(target, returned)
    return result[None]


def solution(mesh):
    placed = (
        P("dp", None, None, "mp", "inner"),
        P("dp", None, None),
        P("dp", "mp", None, None, None),
        P("dp", "mp", None, None, "inner"),
    )
    return jax.shard_map(
        shards, mesh=mesh, in_specs=placed, out_specs=P("dp", None, "mp", "inner"), check_vma=False
    )
```

time: 168 us -> 171 us (1.018)
  blocking collectives: 54.4 us -> 126 us
  waiting for transfers between devices: 61.9 us -> 18.8 us
  starting transfers between devices: 41.2 us -> 13 us
  Pallas kernels: 1.83 us -> 7.63 us
    all_to_all x1 -> x2, blocking collectives: 54.4 us -> 126 us  [the longest x1 71.3 us: shards(): received = lax.all_to_all(outgoing, GROUP_AXES, 0, 0, tiled=True)]
    all_to_all x1 -> x0, waiting for transfers between devices: 44 us -> none  [shards(): received = lax.all_to_all(outgoing, GROUP_AXES, 0, 0, tiled=True)]
    all_to_all x1 -> x0, starting transfers between devices: 28.5 us -> none  [shards(): received = lax.all_to_all(outgoing, GROUP_AXES, 0, 0, tiled=True)]
    pallas_call x1 -> x3, Pallas kernels: 1.83 us -> 7.63 us  [the longest x1 3.17 us: shards(): pl.pallas_call(grafted, out_shape=jax.ShapeDtypeStruct(shape, jnp.bfloat1...]
    reshape x2 -> x0, local copies, waits for them, and re-layouts: 1.77 us -> none  [the longest x1 1.29 us: shards(): outgoing = outgoing.reshape(owners_count * parts, held * row_len, col_len)]
  transfers between devices with their start and end apart: 4 -> 3, of which waited for: 3 -> 2; matrix products, arithmetic and copies ran while one was open for 4% -> 3% of each run, Pallas kernels for 0% -> 0%
where the time goes in v2:
time: 171 us; the launch traced here: 170 us
  blocking collectives  126 us (74%)
  waiting for transfers between devices  18.8 us (11%)
  starting transfers between devices  13 us (8%)
  Pallas kernels  7.63 us (4%)
  local copies, waits for them, and re-layouts  3.75 us (2%)
    all_to_all x1, blocking collectives, shards(): received = lax.all_to_all(outgoing, GROUP_AXES, 0, 0, tiled=True)  71.3 us
    all_to_all x1, blocking collectives, shards(): lax.all_to_all(direction.reshape(sending), GROUP_AXES, 0, 0, tiled=True)  54.6 us
    ppermute x2, waiting for transfers between devices, shards(): terms.append(lax.ppermute(sent, 'dp', ring(replicas, step)))  18.8 us
    ppermute x2, starting transfers between devices, shards(): terms.append(lax.ppermute(sent, 'dp', ring(replicas, step)))  7.99 us
    all_to_all x1, starting transfers between devices, shards(): lax.all_to_all(right_root[0, 0].reshape(parts, held, *right_root.shape[3:...  4.97 us
  transfers between devices with their start and end apart: 3, of which 2 were waited for; matrix products, arithmetic and copies ran while one was open for 3% of the time, Pallas kernels for 0%

profile of v2, /device:TPU:1, one launch (start us, length us, event | category | flops | bytes accessed | tf_op | source)
XLA Modules:
  0.0 170.0 jit_solution(3224540676263219232)
XLA Ops:
  0.0 0.0 copy-start
  0.0 0.0 copy-start.1
  0.0 5.0 %all-to-all-start = ((bf16[4,2,512,128]{3,2,1,0:T(8,128)(2,1)}), bf16[4,2,512,128]{3,2,1,0:T(8,128)(2,1)}, u32[]{:S(2)}, u32[]{:S(2)}) async-start(bf16[4,2,512,128]{3,2,1,0:T(8,128)(2,1)} %bitcast.36), calls=%async_computation | async-start | bytes 2097152 | tf_op jit(solution)/shard_map/all_to_all | solution.py:99
  5.0 2.3 %dynamic-slice_bitcast_fusion.1 = (bf16[256,8,128]{2,1,0:T(8,128)(2,1)}, bf16[256,8,128]{2,1,0:T(8,128)(2,1)}) fusion(bf16[1,3,256,8,128]{4,3,2,1,0:T(8,128)(2,1)} %param.4, s32[]{:T(128)S(6)} %select_n.17, s32[]{:T(128)S(6)} %select_n.16), kind=kLoop, calls=%fused_computation.1 | loop fusion | bytes 2097160 | tf_op jit(solution)/shard_map/jit(dynamic_index_in_dim)/squeeze | solution.py:84
  7.2 6.1 %collective-permute-start.1 = (bf16[256,8,128]{2,1,0:T(8,128)(2,1)}, bf16[256,8,128]{2,1,0:T(8,128)(2,1)S(1)}, u32[]{:S(2)}, u32[]{:S(2)}) collective-permute-start(bf16[256,8,128]{2,1,0:T(8,128)(2,1)} %get-tuple-element.17), channel_id=1, source_target_pairs={{0,512},{256,0},{512,256},{1,513},{257,1},{513,257},{2,514},{258,2... | collective-permute-start | bytes 1572872 | tf_op jit(solution)/shard_map/ppermute | solution.py:85
  13.3 1.9 %collective-permute-start = (bf16[256,8,128]{2,1,0:T(8,128)(2,1)}, bf16[256,8,128]{2,1,0:T(8,128)(2,1)}, u32[]{:S(2)}, u32[]{:S(2)}) collective-permute-start(bf16[256,8,128]{2,1,0:T(8,128)(2,1)} %get-tuple-element.18), channel_id=1, source_target_pairs={{0,256},{256,512},{512,0},{1,257},{257,513},{513,1},{2,258},{258,5... | collective-permute-start | bytes 1572872 | tf_op jit(solution)/shard_map/ppermute | solution.py:85
  15.2 0.0 copy-done.1
  15.3 0.6 reduce-window.6
  15.9 0.2 slice_reduce_fusion
  16.1 0.1 fusion.2
  16.2 0.1 select_reduce_fusion.source_ref
  16.4 1.3 dynamic-slice_bitcast_fusion.left_ref
  17.7 0.0 all-to-all-done.right_ref
  17.7 2.1 %collective-permute-done.1.rest_1_ = bf16[256,8,128]{2,1,0:T(8,128)(2,1)S(1)} collective-permute-done((bf16[256,8,128]{2,1,0:T(8,128)(2,1)}, bf16[256,8,128]{2,1,0:T(8,128)(2,1)S(1)}, u32[]{:S(2)}, u32[]{:S(2)}) %collective-permute-start.1) | collective-permute-done | bytes 524320 | tf_op jit(solution)/shard_map/ppermute | solution.py:85
  19.8 16.8 %collective-permute-done.rest_0_ = bf16[256,8,128]{2,1,0:T(8,128)(2,1)} collective-permute-done((bf16[256,8,128]{2,1,0:T(8,128)(2,1)}, bf16[256,8,128]{2,1,0:T(8,128)(2,1)}, u32[]{:S(2)}, u32[]{:S(2)}) %collective-permute-start) | collective-permute-done | bytes 524320 | tf_op jit(solution)/shard_map/ppermute | solution.py:85
  36.5 0.0 copy-done
  36.5 2.7 %shard_map.46 = bf16[512,8,128]{2,1,0:T(8,128)(2,1)S(1)} custom-call(s32[512]{0:T(512)S(1)} %select_reduce_fusion.source_ref, s32[1]{0:T(128)} %bitcast.5.span_ref, bf16[3,256,8,128]{3,2,1,0:T(8,128)(2,1)S(1)} %bitcast.33, bf16[256,8,128]{2,1,0:T(8,128)(2,1)} %collective-permute-done.rest_0_, bf16[256,8,128]{2,1,0:T(8,128)(2,1)S(1)} %collective-permute-done.1.rest_1_), custom_call_target="tpu_custom_call" | custom-call | tf_op jit(solution)/shard_map/pallas_call | solution.py:107
  39.2 71.3 %all_to_all.15 = bf16[512,8,128]{2,1,0:T(8,128)(2,1)S(1)} all-to-all(bf16[512,8,128]{2,1,0:T(8,128)(2,1)S(1)} %shard_map.46), channel_id=1, replica_groups=mesh['dp'=3,'mp'=64,'inner'=4] {'mp','inner'}, dimensions={0} | all-to-all | bytes 2097152 | tf_op jit(solution)/shard_map/all_to_all | solution.py:121
  110.5 3.2 %shard_map.47 = bf16[64,4,2,8,128]{4,3,2,1,0:T(8,128)(2,1)S(1)} custom-call(bf16[64,4,2,8,128]{4,3,2,1,0:T(8,128)(2,1)S(1)} %bitcast.34, bf16[2,512,512]{2,1,0:T(8,128)(2,1)S(1)} %dynamic-slice_bitcast_fusion.left_ref, bf16[4,2,512,128]{3,2,1,0:T(8,128)(2,1)} %all-to-all-done.right_ref), custom_call_target="tpu_custom_call" | custom-call | tf_op jit(solution)/shard_map/pallas_call | solution.py:123
  113.7 54.6 %all_to_all.16.from_ref = bf16[512,8,128]{2,1,0:T(8,128)(2,1)S(1)} all-to-all(bf16[512,8,128]{2,1,0:T(8,128)(2,1)S(1)} %bitcast.35), channel_id=1, replica_groups=mesh['dp'=3,'mp'=64,'inner'=4] {'mp','inner'}, dimensions={0} | all-to-all | bytes 2097152 | tf_op jit(solution)/shard_map/all_to_all | solution.py:128
  168.2 1.8 %shard_map.48 = bf16[256,8,128]{2,1,0:T(8,128)(2,1)} custom-call(s32[256]{0:T(256)S(1)} %multiply_add_fusion.place_ref, bf16[512,8,128]{2,1,0:T(8,128)(2,1)S(1)} %all_to_all.16.from_ref), custom_call_target="tpu_custom_call" | custom-call | tf_op jit(solution)/shard_map/pallas_call | solution.py:129
  (4 shorter events, 0.1 us)
Async XLA Ops:
  0.0 36.5 %copy-start = (bf16[1,3,256,8,128]{4,3,2,1,0:T(8,128)(2,1)S(1)}, bf16[1,3,256,8,128]{4,3,2,1,0:T(8,128)(2,1)}, u32[]{:S(2)}) copy-start(bf16[1,3,256,8,128]{4,3,2,1,0:T(8,128)(2,1)} %param.4) | copy-start | bytes 4718596
  0.0 15.2 %copy-start.1 = (s32[1,256,1]{1,2,0:T(1,128)S(1)}, s32[1,256,1]{1,2,0:T(1,128)}, u32[]{:S(2)}) copy-start(s32[1,256,1]{1,2,0:T(1,128)} %param.5) | copy-start | bytes 3076
  0.0 17.7 %all-to-all-start = ((bf16[4,2,512,128]{3,2,1,0:T(8,128)(2,1)}), bf16[4,2,512,128]{3,2,1,0:T(8,128)(2,1)}, u32[]{:S(2)}, u32[]{:S(2)}) async-start(bf16[4,2,512,128]{3,2,1,0:T(8,128)(2,1)} %bitcast.36), calls=%async_computation | async-start | bytes 2097152 | tf_op jit(solution)/shard_map/all_to_all | solution.py:99
  7.2 12.5 %collective-permute-start.1 = (bf16[256,8,128]{2,1,0:T(8,128)(2,1)}, bf16[256,8,128]{2,1,0:T(8,128)(2,1)S(1)}, u32[]{:S(2)}, u32[]{:S(2)}) collective-permute-start(bf16[256,8,128]{2,1,0:T(8,128)(2,1)} %get-tuple-element.17), channel_id=1, source_target_pairs={{0,512},{256,0},{512,256},{1,513},{257,1},{513,257},{2,514},{258,2... | collective-permute-start | bytes 1572872 | tf_op jit(solution)/shard_map/ppermute | solution.py:85
  13.3 23.2 %collective-permute-start = (bf16[256,8,128]{2,1,0:T(8,128)(2,1)}, bf16[256,8,128]{2,1,0:T(8,128)(2,1)}, u32[]{:S(2)}, u32[]{:S(2)}) collective-permute-start(bf16[256,8,128]{2,1,0:T(8,128)(2,1)} %get-tuple-element.18), channel_id=1, source_target_pairs={{0,256},{256,512},{512,0},{1,257},{257,513},{513,1},{2,258},{258,5... | collective-permute-start | bytes 1572872 | tf_op jit(solution)/shard_map/ppermute | solution.py:85

commit v3 on v2

v3 whole, which is shorter than its diff:
```python
import jax
import jax.numpy as jnp
from jax import lax
from jax.experimental import pallas as pl
from jax.experimental.pallas import tpu as pltpu
from jax.sharding import PartitionSpec as P

GROUP_AXES = ("mp", "inner")
UNROLL = 8
MIB = 1024 * 1024
IN_SMEM = pl.BlockSpec(memory_space=pltpu.SMEM)
IN_VMEM = pl.BlockSpec(memory_space=pltpu.VMEM)
IN_ANY = pl.BlockSpec(memory_space=pl.ANY)


def ring(size, step):
    return [(i, (i + step) % size) for i in range(size)]


def picked(source_ref, *rest):
    *terms, out_ref, total = rest
    summed = terms[0][...].astype(jnp.float32)
    for term in terms[1:]:
        summed = summed + term[...].astype(jnp.float32)
    total[...] = summed.astype(jnp.bfloat16)
    copied(source_ref, total, out_ref)


def copied(place_ref, from_ref, to_ref):
    def step(turn, carry):
        for offset in range(UNROLL):
            at = turn * UNROLL + offset
            to_ref[at] = from_ref[place_ref[at]]
        return carry

    lax.fori_loop(0, to_ref.shape[0] // UNROLL, step, 0)


def grafted(place_ref, received_ref, left_ref, right_ref, out_ref, left_held, right_held, ready):
    pieces, parts, pair_rows, lanes = received_ref.shape
    held = left_held.shape[0]
    row_len = pair_rows // held
    first = place_ref[0] * held
    left_copy = pltpu.make_async_copy(left_ref.at[pl.ds(first, held)], left_held, ready.at[0])
    right_copy = pltpu.make_async_copy(
        right_ref.at[:, pl.ds(first, held)], right_held, ready.at[1]
    )
    left_copy.start()
    right_copy.start()
    gradients = []
    for slot in range(held):
        rows = slice(slot * row_len, (slot + 1) * row_len)
        gradients.append(
            jnp.concatenate(
                [
                    received_ref[:, part]
                    .astype(jnp.float32)[:, rows]
                    .reshape(pieces * row_len, lanes)
                    for part in range(parts)
                ],
                axis=1,
            )
        )
    left_copy.wait()
    right_copy.wait()
    directions = []
    for slot, gradient in enumerate(gradients):
        left = jnp.dot(
            left_held[slot], gradient.astype(jnp.bfloat16), preferred_element_type=jnp.float32
        ).astype(jnp.bfloat16)
        right = jnp.concatenate([right_held[part, slot] for part in range(parts)], axis=1)
        product = jnp.dot(left, right, preferred_element_type=jnp.float32)
        grad_square = jnp.sum(jnp.square(gradient))
        pre_square = jnp.sum(jnp.square(product))
        factor = jnp.sqrt(jnp.full((1, lanes), grad_square / (pre_square + 1e-06), jnp.float32))
        directions.append(product * factor[:, :1])
    for part in range(parts):
        columns = slice(part * lanes, (part + 1) * lanes)
        out_ref[:, part] = jnp.concatenate(
            [each[:, columns].reshape(pieces, row_len, lanes) for each in directions], axis=1
        ).astype(jnp.bfloat16)


def shards(grads, table, left_root, right_root):
    replicas = lax.axis_size("dp")
    owners_count = lax.axis_size("mp")
    parts = lax.axis_size("inner")
    capacity = left_root.shape[2]
    held = capacity // parts
    _, _, group_len, row_len, col_len = grads.shape
    slot_total = owners_count * capacity
    me = lax.axis_index("dp")
    inner = lax.axis_index("inner")
    params = pltpu.CompilerParams(vmem_limit_bytes=32 * MIB)

    terms = [lax.dynamic_index_in_dim(grads[0], me, 0, keepdims=False)]
    for step in range(1, replicas):
        other = lax.rem(me + step, replicas)
        sent = lax.dynamic_index_in_dim(grads[0], other, 0, keepdims=False)
        terms.append(lax.ppermute(sent, "dp", ring(replicas, step)))
    right = lax.all_gather(right_root[0, 0], "inner", axis=0, tiled=False)

    owner = table[0, :, 0]
    onehot = (owner[:, None] == jnp.arange(owners_count, dtype=jnp.int32)[None, :]).astype(
        jnp.int32
    )
    rank = jnp.sum((jnp.cumsum(onehot, axis=0) - onehot) * onehot, axis=1)
    target = owner * capacity + rank
    slots = jnp.arange(slot_total, dtype=jnp.int32)
    blocks = jnp.arange(group_len, dtype=jnp.int32)
    source = jnp.sum(
        jnp.where(target[None, :] == slots[:, None], blocks[None, :], 0), axis=1
    ).astype(jnp.int32)

    piece = (group_len, row_len, col_len)
    sending = (slot_total, row_len, col_len)
    paired = (owners_count * parts, held * row_len, col_len)
    outgoing = pl.pallas_call(
        picked,
        in_specs=[IN_SMEM] + [IN_VMEM] * replicas,
        out_specs=IN_VMEM,
        out_shape=jax.ShapeDtypeStruct(sending, jnp.bfloat16),
        scratch_shapes=[pltpu.VMEM(piece, jnp.bfloat16)],
        compiler_params=params,
    )(source, *terms)
    received = lax.all_to_all(outgoing.reshape(paired), GROUP_AXES, 0, 0, tiled=True)
    shape = (owners_count, parts, held * row_len, col_len)
    direction = pl.pallas_call(
        grafted,
        in_specs=[IN_SMEM, IN_VMEM, IN_ANY, IN_ANY],
        out_specs=IN_VMEM,
        out_shape=jax.ShapeDtypeStruct(shape, jnp.bfloat16),
        scratch_shapes=[
            pltpu.VMEM((held, *left_root.shape[3:]), jnp.bfloat16),
            pltpu.VMEM((parts, held, *right_root.shape[3:]), jnp.bfloat16),
            pltpu.SemaphoreType.DMA((2,)),
        ],
        compiler_params=pltpu.CompilerParams(vmem_limit_bytes=50 * MIB),
    )(jnp.full((1,), inner, jnp.int32), received.reshape(shape), left_root[0, 0], right)
    returned = lax.all_to_all(direction.reshape(paired), GROUP_AXES, 0, 0, tiled=True)
    result = pl.pallas_call(
        copied,
        in_specs=[IN_SMEM, IN_VMEM],
        out_specs=IN_VMEM,
        out_shape=jax.ShapeDtypeStruct(piece, jnp.bfloat16),
        compiler_params=params,
    )(target, returned.reshape(sending))
    return result[None]


def solution(mesh):
    placed = (
        P("dp", None, None, "mp", "inner"),
        P("dp", None, None),
        P("dp", "mp", None, None, None),
        P("dp", "mp", None, None, "inner"),
    )
    return jax.shard_map(
        shards, mesh=mesh, in_specs=placed, out_specs=P("dp", None, "mp", "inner"), check_vma=False
    )
```

time: 171 us -> 179 us (1.047)
  blocking collectives: 126 us -> 54.4 us
  waiting for transfers between devices: 18.8 us -> 63 us
  starting transfers between devices: 13 us -> 37.3 us
  between operations: 0.08 us -> 13.5 us
  local copies, waits for them, and re-layouts: 3.75 us -> 1.66 us
    all_to_all x2 -> x1, blocking collectives: 126 us -> 54.4 us  [shards(): lax.all_to_all(direction.reshape(paired), GROUP_AXES, 0, 0, tiled=True)]
    all_to_all x1, waiting for transfers between devices: 0.01 us -> 45.3 us  [shards(): lax.all_to_all(outgoing.reshape(paired), GROUP_AXES, 0, 0, tiled=True)]
    all_to_all x1, starting transfers between devices: 4.97 us -> 28.7 us  [shards(): lax.all_to_all(outgoing.reshape(paired), GROUP_AXES, 0, 0, tiled=True)]
    ppermute x2, waiting for transfers between devices: 18.8 us -> 17 us  [shards(): terms.append(lax.ppermute(sent, 'dp', ring(replicas, step)))]
  transfers between devices with their start and end apart: 3 -> 4, of which waited for: 2 -> 3; matrix products, arithmetic and copies ran while one was open for 3% -> 1% of each run, Pallas kernels for 0% -> 1%
where the time goes in v3:
time: 179 us
  waiting for transfers between devices  63 us (35%)
  blocking collectives  54.4 us (30%)
  starting transfers between devices  37.3 us (21%)
  between operations  13.5 us (8%)
  Pallas kernels  7.82 us (4%)
    all_to_all x1, blocking collectives, shards(): lax.all_to_all(direction.reshape(paired), GROUP_AXES, 0, 0, tiled=True)  54.4 us
    all_to_all x1, waiting for transfers between devices, shards(): lax.all_to_all(outgoing.reshape(paired), GROUP_AXES, 0, 0, tiled=True)  45.3 us
    all_to_all x1, starting transfers between devices, shards(): lax.all_to_all(outgoing.reshape(paired), GROUP_AXES, 0, 0, tiled=True)  28.7 us
    ppermute x2, waiting for transfers between devices, shards(): terms.append(lax.ppermute(sent, 'dp', ring(replicas, step)))  17 us
    ppermute x2, starting transfers between devices, shards(): terms.append(lax.ppermute(sent, 'dp', ring(replicas, step)))  8.56 us
  transfers between devices with their start and end apart: 4, of which 3 were waited for; matrix products, arithmetic and copies ran while one was open for 1% of the time, Pallas kernels for 1%

profile of v3, /device:TPU:1, one launch (start us, length us, event | category | flops | bytes accessed | tf_op | source)
XLA Modules:
  0.0 178.6 jit_solution(15339384139417640440)
XLA Ops:
  6.5 0.0 copy-start
  6.5 0.0 all-gather.3.cloned.1.call-start
  6.5 0.7 all-gather.3.cloned.1.call-update
  7.3 1.5 dynamic-slice_bitcast_fusion
  8.8 4.8 %collective-permute-start = (bf16[256,8,128]{2,1,0:T(8,128)(2,1)S(1)}, bf16[256,8,128]{2,1,0:T(8,128)(2,1)S(1)}, u32[]{:S(2)}, u32[]{:S(2)}) collective-permute-start(bf16[256,8,128]{2,1,0:T(8,128)(2,1)S(1)} %get-tuple-element.7), channel_id=1, source_target_pairs={{0,256},{256,512},{512,0},{1,257},{257,513},{513,1},{2,258},{258,5... | collective-permute-start | bytes 1572872 | tf_op jit(solution)/shard_map/ppermute | solution.py:100
  13.6 3.7 %collective-permute-start.1 = (bf16[256,8,128]{2,1,0:T(8,128)(2,1)S(1)}, bf16[256,8,128]{2,1,0:T(8,128)(2,1)S(1)}, u32[]{:S(2)}, u32[]{:S(2)}) collective-permute-start(bf16[256,8,128]{2,1,0:T(8,128)(2,1)S(1)} %get-tuple-element.5), channel_id=1, source_target_pairs={{0,512},{256,0},{512,256},{1,513},{257,1},{513,257},{2,514},{258,2... | collective-permute-start | bytes 1572872 | tf_op jit(solution)/shard_map/ppermute | solution.py:100
  17.3 0.0 copy-done
  17.4 0.6 reduce-window.6
  18.0 0.2 slice_reduce_fusion
  18.2 0.1 fusion.2
  18.3 0.2 select_reduce_fusion.source_ref
  18.5 3.6 %collective-permute-done.rest_1_ = bf16[256,8,128]{2,1,0:T(8,128)(2,1)S(1)} collective-permute-done((bf16[256,8,128]{2,1,0:T(8,128)(2,1)S(1)}, bf16[256,8,128]{2,1,0:T(8,128)(2,1)S(1)}, u32[]{:S(2)}, u32[]{:S(2)}) %collective-permute-start) | collective-permute-done | bytes 524320 | tf_op jit(solution)/shard_map/ppermute | solution.py:100
  22.1 13.4 %collective-permute-done.1.rest_2_ = bf16[256,8,128]{2,1,0:T(8,128)(2,1)S(1)} collective-permute-done((bf16[256,8,128]{2,1,0:T(8,128)(2,1)S(1)}, bf16[256,8,128]{2,1,0:T(8,128)(2,1)S(1)}, u32[]{:S(2)}, u32[]{:S(2)}) %collective-permute-start.1) | collective-permute-done | bytes 524320 | tf_op jit(solution)/shard_map/ppermute | solution.py:100
  35.5 2.6 %shard_map.46 = bf16[512,8,128]{2,1,0:T(8,128)(2,1)} custom-call(s32[512]{0:T(512)S(1)} %select_reduce_fusion.source_ref, bf16[256,8,128]{2,1,0:T(8,128)(2,1)S(1)} %get-tuple-element.6.rest_0_, bf16[256,8,128]{2,1,0:T(8,128)(2,1)S(1)} %collective-permute-done.rest_1_, bf16[256,8,128]{2,1,0:T(8,128)(2,1)S(1)} %collective-permute-done.1.rest_2_), custom_call_target="tpu_custom_call" | custom-call | tf_op jit(solution)/shard_map/pallas_call | solution.py:118
  38.1 28.7 %all-to-all-start = ((bf16[256,16,128]{2,1,0:T(8,128)(2,1)}), bf16[256,16,128]{2,1,0:T(8,128)(2,1)S(1)}, u32[]{:S(2)}, u32[]{:S(2)}) async-start(bf16[256,16,128]{2,1,0:T(8,128)(2,1)} %bitcast.7), calls=%async_computation | async-start | bytes 2097152 | tf_op jit(solution)/shard_map/all_to_all | solution.py:126
  66.9 45.3 %all-to-all-done = bf16[256,16,128]{2,1,0:T(8,128)(2,1)S(1)} async-done(((bf16[256,16,128]{2,1,0:T(8,128)(2,1)}), bf16[256,16,128]{2,1,0:T(8,128)(2,1)S(1)}, u32[]{:S(2)}, u32[]{:S(2)}) %all-to-all-start) | async-done | bytes 1048608 | tf_op jit(solution)/shard_map/all_to_all | solution.py:126
  112.2 0.0 all-gather.3.cloned.1.call-done
  112.2 3.4 %shard_map.47 = bf16[64,4,16,128]{3,2,1,0:T(8,128)(2,1)S(1)} custom-call(s32[1]{0:T(128)} %bitcast.3.place_ref, bf16[64,4,16,128]{3,2,1,0:T(8,128)(2,1)S(1)} %bitcast.36, bf16[8,512,512]{2,1,0:T(8,128)(2,1)} %bitcast.38, bf16[4,8,512,128]{3,2,1,0:T(8,128)(2,1)} %bitcast.39), custom_call_target="tpu_custom_call" | custom-call | tf_op jit(solution)/shard_map/pallas_call | solution.py:128
  115.6 54.4 %all_to_all.10 = bf16[256,16,128]{2,1,0:T(8,128)(2,1)S(1)} all-to-all(bf16[256,16,128]{2,1,0:T(8,128)(2,1)S(1)} %bitcast.37), channel_id=1, replica_groups=mesh['dp'=3,'mp'=64,'inner'=4] {'mp','inner'}, dimensions={0} | all-to-all | bytes 2097152 | tf_op jit(solution)/shard_map/all_to_all | solution.py:140
  169.9 1.8 %shard_map.48 = bf16[256,8,128]{2,1,0:T(8,128)(2,1)} custom-call(s32[256]{0:T(256)S(1)} %multiply_add_fusion.place_ref, bf16[512,8,128]{2,1,0:T(8,128)(2,1)S(1)} %bitcast.35), custom_call_target="tpu_custom_call" | custom-call | tf_op jit(solution)/shard_map/pallas_call | solution.py:141
  (4 shorter events, 0.1 us)
Async XLA Ops:
  6.5 10.8 %copy-start = (s32[1,256,1]{1,2,0:T(1,128)S(1)}, s32[1,256,1]{1,2,0:T(1,128)}, u32[]{:S(2)}) copy-start(s32[1,256,1]{1,2,0:T(1,128)} %param.5) | copy-start | bytes 3076
  6.5 105.6 %all-gather.3.cloned.1.call-start = ((), (), s32[]{:S(2)}) async-start(), calls=%async_computation.2 | async-start | bytes 5242880 | tf_op jit(solution)/shard_map/all_gather | solution.py:101
  8.8 13.3 %collective-permute-start = (bf16[256,8,128]{2,1,0:T(8,128)(2,1)S(1)}, bf16[256,8,128]{2,1,0:T(8,128)(2,1)S(1)}, u32[]{:S(2)}, u32[]{:S(2)}) collective-permute-start(bf16[256,8,128]{2,1,0:T(8,128)(2,1)S(1)} %get-tuple-element.7), channel_id=1, source_target_pairs={{0,256},{256,512},{512,0},{1,257},{257,513},{513,1},{2,258},{258,5... | collective-permute-start | bytes 1572872 | tf_op jit(solution)/shard_map/ppermute | solution.py:100
  13.6 21.9 %collective-permute-start.1 = (bf16[256,8,128]{2,1,0:T(8,128)(2,1)S(1)}, bf16[256,8,128]{2,1,0:T(8,128)(2,1)S(1)}, u32[]{:S(2)}, u32[]{:S(2)}) collective-permute-start(bf16[256,8,128]{2,1,0:T(8,128)(2,1)S(1)} %get-tuple-element.5), channel_id=1, source_target_pairs={{0,512},{256,0},{512,256},{1,513},{257,1},{513,257},{2,514},{258,2... | collective-permute-start | bytes 1572872 | tf_op jit(solution)/shard_map/ppermute | solution.py:100
  38.1 74.0 %all-to-all-start = ((bf16[256,16,128]{2,1,0:T(8,128)(2,1)}), bf16[256,16,128]{2,1,0:T(8,128)(2,1)S(1)}, u32[]{:S(2)}, u32[]{:S(2)}) async-start(bf16[256,16,128]{2,1,0:T(8,128)(2,1)} %bitcast.7), calls=%async_computation | async-start | bytes 2097152 | tf_op jit(solution)/shard_map/all_to_all | solution.py:126
Sparse Core Ops, SparseCore 0:
  9.7 65.7 all-gather.2

commit v4 on v3

--- a/solution.py
+++ b/solution.py
@@ -6,11 +6,10 @@
 from jax.sharding import PartitionSpec as P
 
 GROUP_AXES = ("mp", "inner")
-UNROLL = 8
+UNROLL = 16
 MIB = 1024 * 1024
 IN_SMEM = pl.BlockSpec(memory_space=pltpu.SMEM)
 IN_VMEM = pl.BlockSpec(memory_space=pltpu.VMEM)
-IN_ANY = pl.BlockSpec(memory_space=pl.ANY)
 
 
 def ring(size, step):
@@ -36,39 +35,26 @@
     lax.fori_loop(0, to_ref.shape[0] // UNROLL, step, 0)
 
 
-def grafted(place_ref, received_ref, left_ref, right_ref, out_ref, left_held, right_held, ready):
+def grafted(received_ref, left_ref, right_ref, out_ref):
     pieces, parts, pair_rows, lanes = received_ref.shape
-    held = left_held.shape[0]
+    held = left_ref.shape[0]
     row_len = pair_rows // held
-    first = place_ref[0] * held
-    left_copy = pltpu.make_async_copy(left_ref.at[pl.ds(first, held)], left_held, ready.at[0])
-    right_copy = pltpu.make_async_copy(
-        right_ref.at[:, pl.ds(first, held)], right_held, ready.at[1]
-    )
-    left_copy.start()
-    right_copy.start()
-    gradients = []
+    directions = []
     for slot in range(held):
         rows = slice(slot * row_len, (slot + 1) * row_len)
-        gradients.append(
-            jnp.concatenate(
-                [
-                    received_ref[:, part]
-                    .astype(jnp.float32)[:, rows]
-                    .reshape(pieces * row_len, lanes)
-                    for part in range(parts)
-                ],
-                axis=1,
-            )
+        gradient = jnp.concatenate(
+            [
+                received_ref[:, part]
+                .astype(jnp.float32)[:, rows]
+                .reshape(pieces * row_len, lanes)
+                for part in range(parts)
+            ],
+            axis=1,
         )
-    left_copy.wait()
-    right_copy.wait()
-    directions = []
-    for slot, gradient in enumerate(gradients):
         left = jnp.dot(
-            left_held[slot], gradient.astype(jnp.bfloat16), preferred_element_type=jnp.float32
+            left_ref[slot], gradient.astype(jnp.bfloat16), preferred_element_type=jnp.float32
         ).astype(jnp.bfloat16)
-        right = jnp.concatenate([right_held[part, slot] for part in range(parts)], axis=1)
+        right = jnp.concatenate([right_ref[part, slot] for part in range(parts)], axis=1)
         product = jnp.dot(left, right, preferred_element_type=jnp.float32)
         grad_square = jnp.sum(jnp.square(gradient))
         pre_square = jnp.sum(jnp.square(product))
@@ -98,7 +84,11 @@
         other = lax.rem(me + step, replicas)
         sent = lax.dynamic_index_in_dim(grads[0], other, 0, keepdims=False)
         terms.append(lax.ppermute(sent, "dp", ring(replicas, step)))
-    right = lax.all_gather(right_root[0, 0], "inner", axis=0, tiled=False)
+    right = lax.all_to_all(
+        right_root[0, 0].reshape(parts, held, *right_root.shape[3:]), "inner", 0, 0, tiled=True
+    )
+
+    left = lax.dynamic_slice_in_dim(left_root[0, 0], inner * held, held, 0)
 
     owner = table[0, :, 0]
     onehot = (owner[:, None] == jnp.arange(owners_count, dtype=jnp.int32)[None, :]).astype(
@@ -127,16 +117,11 @@
     shape = (owners_count, parts, held * row_len, col_len)
     direction = pl.pallas_call(
         grafted,
-        in_specs=[IN_SMEM, IN_VMEM, IN_ANY, IN_ANY],
+        in_specs=[IN_VMEM] * 3,
         out_specs=IN_VMEM,
         out_shape=jax.ShapeDtypeStruct(shape, jnp.bfloat16),
-        scratch_shapes=[
-            pltpu.VMEM((held, *left_root.shape[3:]), jnp.bfloat16),
-            pltpu.VMEM((parts, held, *right_root.shape[3:]), jnp.bfloat16),
-            pltpu.SemaphoreType.DMA((2,)),
-        ],
-        compiler_params=pltpu.CompilerParams(vmem_limit_bytes=50 * MIB),
-    )(jnp.full((1,), inner, jnp.int32), received.reshape(shape), left_root[0, 0], right)
+        compiler_params=params,
+    )(received.reshape(shape), left, right)
     returned = lax.all_to_all(direction.reshape(paired), GROUP_AXES, 0, 0, tiled=True)
     result = pl.pallas_call(
         copied,

time: 179 us -> 164 us (0.916)
  between operations: 13.5 us -> 0.07 us
  waiting for transfers between devices: 63 us -> 57.3 us
  starting transfers between devices: 37.3 us -> 41.2 us
  local copies, waits for them, and re-layouts: 1.66 us -> 3.75 us
  Pallas kernels: 7.82 us -> 5.99 us
    all_to_all x0 -> x1, starting transfers between devices: none -> 4.02 us  [shards(): lax.all_to_all(right_root[0, 0].reshape(parts, held, *right_root.shape[3:...]
    ppermute x2, waiting for transfers between devices: 17 us -> 13.3 us  [shards(): terms.append(lax.ppermute(sent, 'dp', ring(replicas, step)))]
  transfers between devices with their start and end apart: 4 -> 4, of which waited for: 3 -> 2; matrix products, arithmetic and copies ran while one was open for 1% -> 1% of each run, Pallas kernels for 1% -> 1%
where the time goes in v4:
time: 164 us
  waiting for transfers between devices  57.3 us (35%)
  blocking collectives  54.4 us (33%)
  starting transfers between devices  41.2 us (25%)
  Pallas kernels  5.99 us (4%)
  local copies, waits for them, and re-layouts  3.75 us (2%)
    all_to_all x1, blocking collectives, shards(): lax.all_to_all(direction.reshape(paired), GROUP_AXES, 0, 0, tiled=True)  54.4 us
    all_to_all x1, waiting for transfers between devices, shards(): lax.all_to_all(outgoing.reshape(paired), GROUP_AXES, 0, 0, tiled=True)  44 us
    all_to_all x1, starting transfers between devices, shards(): lax.all_to_all(outgoing.reshape(paired), GROUP_AXES, 0, 0, tiled=True)  28.6 us
    ppermute x2, waiting for transfers between devices, shards(): terms.append(lax.ppermute(sent, 'dp', ring(replicas, step)))  13.3 us
    ppermute x2, starting transfers between devices, shards(): terms.append(lax.ppermute(sent, 'dp', ring(replicas, step)))  8.55 us
    all_to_all x1, starting transfers between devices, shards(): lax.all_to_all(right_root[0, 0].reshape(parts, held, *right_root.shape[3:...  4.02 us
  transfers between devices with their start and end apart: 4, of which 2 were waited for; matrix products, arithmetic and copies ran while one was open for 1% of the time, Pallas kernels for 1%

profile of v4, /device:TPU:1, one launch (start us, length us, event | category | flops | bytes accessed | tf_op | source)
XLA Modules:
  0.0 163.6 jit_solution(17631390749405024970)
XLA Ops:
  0.0 0.0 copy-start
  0.0 2.3 %dynamic-slice_bitcast_fusion.1 = (bf16[256,8,128]{2,1,0:T(8,128)(2,1)S(1)}, bf16[256,8,128]{2,1,0:T(8,128)(2,1)S(1)}, bf16[256,8,128]{2,1,0:T(8,128)(2,1)}) fusion(bf16[1,3,256,8,128]{4,3,2,1,0:T(8,128)(2,1)} %param.4, s32[]{:T(128)S(6)} %select_n.20, s32[]{:T(128)S(6)} %select_n.18, s32[]{:T(128)S(6)} %select_n.19), kind=kLoop, calls=%fused_computation.1 | loop fusion | bytes 3145740 | tf_op jit(solution)/shard_map/jit(dynamic_index_in_dim)/squeeze | solution.py:85
  2.3 4.8 %collective-permute-start = (bf16[256,8,128]{2,1,0:T(8,128)(2,1)}, bf16[256,8,128]{2,1,0:T(8,128)(2,1)S(1)}, u32[]{:S(2)}, u32[]{:S(2)}) collective-permute-start(bf16[256,8,128]{2,1,0:T(8,128)(2,1)} %get-tuple-element.7), channel_id=1, source_target_pairs={{0,256},{256,512},{512,0},{1,257},{257,513},{513,1},{2,258},{258,5... | collective-permute-start | bytes 1572872 | tf_op jit(solution)/shard_map/ppermute | solution.py:86
  7.1 3.7 %collective-permute-start.1 = (bf16[256,8,128]{2,1,0:T(8,128)(2,1)S(1)}, bf16[256,8,128]{2,1,0:T(8,128)(2,1)S(1)}, u32[]{:S(2)}, u32[]{:S(2)}) collective-permute-start(bf16[256,8,128]{2,1,0:T(8,128)(2,1)S(1)} %get-tuple-element.5), channel_id=1, source_target_pairs={{0,512},{256,0},{512,256},{1,513},{257,1},{513,257},{2,514},{258,2... | collective-permute-start | bytes 1572872 | tf_op jit(solution)/shard_map/ppermute | solution.py:86
  10.8 4.0 %all-to-all-start.1 = ((bf16[4,2,512,128]{3,2,1,0:T(8,128)(2,1)}), bf16[4,2,512,128]{3,2,1,0:T(8,128)(2,1)S(1)}, u32[]{:S(2)}, u32[]{:S(2)}) async-start(bf16[4,2,512,128]{3,2,1,0:T(8,128)(2,1)} %bitcast.38), calls=%async_computation.1 | async-start | bytes 2097152 | tf_op jit(solution)/shard_map/all_to_all | solution.py:87
  14.9 0.0 copy-done
  14.9 0.6 reduce-window.6
  15.5 0.2 slice_reduce_fusion
  15.7 0.1 fusion.2
  15.8 0.2 select_reduce_fusion.source_ref
  16.0 0.0 collective-permute-done.rest_1_
  16.0 13.3 %collective-permute-done.1.rest_2_ = bf16[256,8,128]{2,1,0:T(8,128)(2,1)S(1)} collective-permute-done((bf16[256,8,128]{2,1,0:T(8,128)(2,1)S(1)}, bf16[256,8,128]{2,1,0:T(8,128)(2,1)S(1)}, u32[]{:S(2)}, u32[]{:S(2)}) %collective-permute-start.1) | collective-permute-done | bytes 524320 | tf_op jit(solution)/shard_map/ppermute | solution.py:86
  29.3 2.5 %shard_map.46 = bf16[512,8,128]{2,1,0:T(8,128)(2,1)} custom-call(s32[512]{0:T(512)S(1)} %select_reduce_fusion.source_ref, bf16[256,8,128]{2,1,0:T(8,128)(2,1)S(1)} %get-tuple-element.6.rest_0_, bf16[256,8,128]{2,1,0:T(8,128)(2,1)S(1)} %collective-permute-done.rest_1_, bf16[256,8,128]{2,1,0:T(8,128)(2,1)S(1)} %collective-permute-done.1.rest_2_), custom_call_target="tpu_custom_call" | custom-call | tf_op jit(solution)/shard_map/pallas_call | solution.py:108
  31.8 0.0 all-to-all-done.1.right_ref
  31.8 28.6 %all-to-all-start = ((bf16[256,16,128]{2,1,0:T(8,128)(2,1)}), bf16[256,16,128]{2,1,0:T(8,128)(2,1)S(1)}, u32[]{:S(2)}, u32[]{:S(2)}) async-start(bf16[256,16,128]{2,1,0:T(8,128)(2,1)} %bitcast.6), calls=%async_computation | async-start | bytes 2097152 | tf_op jit(solution)/shard_map/all_to_all | solution.py:116
  60.4 1.3 dynamic-slice_bitcast_fusion.left_ref
  61.7 44.0 %all-to-all-done = bf16[256,16,128]{2,1,0:T(8,128)(2,1)S(1)} async-done(((bf16[256,16,128]{2,1,0:T(8,128)(2,1)}), bf16[256,16,128]{2,1,0:T(8,128)(2,1)S(1)}, u32[]{:S(2)}, u32[]{:S(2)}) %all-to-all-start) | async-done | bytes 1048608 | tf_op jit(solution)/shard_map/all_to_all | solution.py:116
  105.7 1.8 %shard_map.47 = bf16[64,4,16,128]{3,2,1,0:T(8,128)(2,1)S(1)} custom-call(bf16[64,4,16,128]{3,2,1,0:T(8,128)(2,1)S(1)} %bitcast.36, bf16[2,512,512]{2,1,0:T(8,128)(2,1)S(1)} %dynamic-slice_bitcast_fusion.left_ref, bf16[4,2,512,128]{3,2,1,0:T(8,128)(2,1)S(1)} %all-to-all-done.1.right_ref), custom_call_target="tpu_custom_call" | custom-call | tf_op jit(solution)/shard_map/pallas_call | solution.py:118
  107.5 54.4 %all_to_all.15 = bf16[256,16,128]{2,1,0:T(8,128)(2,1)S(1)} all-to-all(bf16[256,16,128]{2,1,0:T(8,128)(2,1)S(1)} %bitcast.37), channel_id=1, replica_groups=mesh['dp'=3,'mp'=64,'inner'=4] {'mp','inner'}, dimensions={0} | all-to-all | bytes 2097152 | tf_op jit(solution)/shard_map/all_to_all | solution.py:125
  161.9 1.7 %shard_map.48 = bf16[256,8,128]{2,1,0:T(8,128)(2,1)} custom-call(s32[256]{0:T(256)S(1)} %multiply_add_fusion.place_ref, bf16[512,8,128]{2,1,0:T(8,128)(2,1)S(1)} %bitcast.35), custom_call_target="tpu_custom_call" | custom-call | tf_op jit(solution)/shard_map/pallas_call | solution.py:126
  (4 shorter events, 0.1 us)
Async XLA Ops:
  0.0 14.9 %copy-start = (s32[1,256,1]{1,2,0:T(1,128)S(1)}, s32[1,256,1]{1,2,0:T(1,128)}, u32[]{:S(2)}) copy-start(s32[1,256,1]{1,2,0:T(1,128)} %param.5) | copy-start | bytes 3076
  2.3 13.7 %collective-permute-start = (bf16[256,8,128]{2,1,0:T(8,128)(2,1)}, bf16[256,8,128]{2,1,0:T(8,128)(2,1)S(1)}, u32[]{:S(2)}, u32[]{:S(2)}) collective-permute-start(bf16[256,8,128]{2,1,0:T(8,128)(2,1)} %get-tuple-element.7), channel_id=1, source_target_pairs={{0,256},{256,512},{512,0},{1,257},{257,513},{513,1},{2,258},{258,5... | collective-permute-start | bytes 1572872 | tf_op jit(solution)/shard_map/ppermute | solution.py:86
  7.1 22.2 %collective-permute-start.1 = (bf16[256,8,128]{2,1,0:T(8,128)(2,1)S(1)}, bf16[256,8,128]{2,1,0:T(8,128)(2,1)S(1)}, u32[]{:S(2)}, u32[]{:S(2)}) collective-permute-start(bf16[256,8,128]{2,1,0:T(8,128)(2,1)S(1)} %get-tuple-element.5), channel_id=1, source_target_pairs={{0,512},{256,0},{512,256},{1,513},{257,1},{513,257},{2,514},{258,2... | collective-permute-start | bytes 1572872 | tf_op jit(solution)/shard_map/ppermute | solution.py:86
  10.8 21.0 %all-to-all-start.1 = ((bf16[4,2,512,128]{3,2,1,0:T(8,128)(2,1)}), bf16[4,2,512,128]{3,2,1,0:T(8,128)(2,1)S(1)}, u32[]{:S(2)}, u32[]{:S(2)}) async-start(bf16[4,2,512,128]{3,2,1,0:T(8,128)(2,1)} %bitcast.38), calls=%async_computation.1 | async-start | bytes 2097152 | tf_op jit(solution)/shard_map/all_to_all | solution.py:87
  31.8 73.9 %all-to-all-start = ((bf16[256,16,128]{2,1,0:T(8,128)(2,1)}), bf16[256,16,128]{2,1,0:T(8,128)(2,1)S(1)}, u32[]{:S(2)}, u32[]{:S(2)}) async-start(bf16[256,16,128]{2,1,0:T(8,128)(2,1)} %bitcast.6), calls=%async_computation | async-start | bytes 2097152 | tf_op jit(solution)/shard_map/all_to_all | solution.py:116

commit v5 on v4

--- a/solution.py
+++ b/solution.py
@@ -10,19 +10,40 @@
 MIB = 1024 * 1024
 IN_SMEM = pl.BlockSpec(memory_space=pltpu.SMEM)
 IN_VMEM = pl.BlockSpec(memory_space=pltpu.VMEM)
+IN_ANY = pl.BlockSpec(memory_space=pl.ANY)
 
 
 def ring(size, step):
     return [(i, (i + step) % size) for i in range(size)]
 
 
-def picked(source_ref, *rest):
-    *terms, out_ref, total = rest
-    summed = terms[0][...].astype(jnp.float32)
-    for term in terms[1:]:
-        summed = summed + term[...].astype(jnp.float32)
-    total[...] = summed.astype(jnp.bfloat16)
-    copied(source_ref, total, out_ref)
+def spans(grads_ref, *rest):
+    *out_refs, ready = rest
+    me = lax.axis_index("dp")
+    copies = []
+    for step, out_ref in enumerate(out_refs):
+        span = lax.rem(me + step, len(out_refs))
+        copies.append(pltpu.make_async_copy(grads_ref.at[span], out_ref, ready.at[step]))
+    for copy in copies:
+        copy.start()
+    for copy in copies:
+        copy.wait()
+
+
+def summed_into_slots(target_ref, *rest):
+    *terms, out_ref = rest
+    out_ref[...] = jnp.zeros_like(out_ref)
+
+    def step(turn, carry):
+        for offset in range(UNROLL):
+            block = turn * UNROLL + offset
+            summed = terms[0][block].astype(jnp.float32)
+            for term in terms[1:]:
+                summed = summed + term[block].astype(jnp.float32)
+            out_ref[target_ref[block]] = summed.astype(jnp.bfloat16)
+        return carry
+
+    lax.fori_loop(0, terms[0].shape[0] // UNROLL, step, 0)
 
 
 def copied(place_ref, from_ref, to_ref):
@@ -75,15 +96,22 @@
     held = capacity // parts
     _, _, group_len, row_len, col_len = grads.shape
     slot_total = owners_count * capacity
-    me = lax.axis_index("dp")
     inner = lax.axis_index("inner")
     params = pltpu.CompilerParams(vmem_limit_bytes=32 * MIB)
 
-    terms = [lax.dynamic_index_in_dim(grads[0], me, 0, keepdims=False)]
-    for step in range(1, replicas):
-        other = lax.rem(me + step, replicas)
-        sent = lax.dynamic_index_in_dim(grads[0], other, 0, keepdims=False)
-        terms.append(lax.ppermute(sent, "dp", ring(replicas, step)))
+    piece = (group_len, row_len, col_len)
+    own, *sent = pl.pallas_call(
+        spans,
+        in_specs=[IN_ANY],
+        out_specs=[IN_VMEM] * replicas,
+        out_shape=[jax.ShapeDtypeStruct(piece, jnp.bfloat16)] * replicas,
+        scratch_shapes=[pltpu.SemaphoreType.DMA((replicas,))],
+        compiler_params=pltpu.CompilerParams(vmem_limit_bytes=50 * MIB),
+    )(grads[0])
+    terms = [own] + [
+        lax.ppermute(each, "dp", ring(replicas, step)) for step, each in enumerate(sent, 1)
+    ]
+    terms[1], right_root = lax.optimization_barrier((terms[1], right_root))
     right = lax.all_to_all(
         right_root[0, 0].reshape(parts, held, *right_root.shape[3:]), "inner", 0, 0, tiled=True
     )
@@ -96,23 +124,15 @@
     )
     rank = jnp.sum((jnp.cumsum(onehot, axis=0) - onehot) * onehot, axis=1)
     target = owner * capacity + rank
-    slots = jnp.arange(slot_total, dtype=jnp.int32)
-    blocks = jnp.arange(group_len, dtype=jnp.int32)
-    source = jnp.sum(
-        jnp.where(target[None, :] == slots[:, None], blocks[None, :], 0), axis=1
-    ).astype(jnp.int32)
-
-    piece = (group_len, row_len, col_len)
     sending = (slot_total, row_len, col_len)
     paired = (owners_count * parts, held * row_len, col_len)
     outgoing = pl.pallas_call(
-        picked,
+        summed_into_slots,
         in_specs=[IN_SMEM] + [IN_VMEM] * replicas,
         out_specs=IN_VMEM,
         out_shape=jax.ShapeDtypeStruct(sending, jnp.bfloat16),
-        scratch_shapes=[pltpu.VMEM(piece, jnp.bfloat16)],
         compiler_params=params,
-    )(source, *terms)
+    )(target, *terms)
     received = lax.all_to_all(outgoing.reshape(paired), GROUP_AXES, 0, 0, tiled=True)
     shape = (owners_count, parts, held * row_len, col_len)
     direction = pl.pallas_call(

time: 164 us -> 173 us (1.055); the launches traced: 164 us -> 171 us
  starting transfers between devices: 41.2 us -> 45.9 us
  other arithmetic: 0.93 us -> 2.8 us
    all_to_all x1, starting transfers between devices: 4.02 us -> 9.09 us  [shards(): lax.all_to_all(right_root[0, 0].reshape(parts, held, *right_root.shape[3:...]
    squeeze x1 -> x0, local copies, waits for them, and re-layouts: 2.26 us -> none  [shards(): sent = lax.dynamic_index_in_dim(grads[0], other, 0, keepdims=False)]
  transfers between devices with their start and end apart: 4 -> 4, of which waited for: 2 -> 3; matrix products, arithmetic and copies ran while one was open for 1% -> 3% of each run, Pallas kernels for 1% -> 1%
where the time goes in v5:
time: 173 us; the launch traced here: 171 us
  waiting for transfers between devices  58.7 us (34%)
  blocking collectives  54.6 us (32%)
  starting transfers between devices  45.9 us (27%)
  Pallas kernels  5.7 us (3%)
  local copies, waits for them, and re-layouts  2.89 us (2%)
  other arithmetic  2.8 us (2%)
    all_to_all x1, blocking collectives, shards(): lax.all_to_all(direction.reshape(paired), GROUP_AXES, 0, 0, tiled=True)  54.6 us
    all_to_all x1, waiting for transfers between devices, shards(): lax.all_to_all(outgoing.reshape(paired), GROUP_AXES, 0, 0, tiled=True)  44.4 us
    all_to_all x1, starting transfers between devices, shards(): lax.all_to_all(outgoing.reshape(paired), GROUP_AXES, 0, 0, tiled=True)  29 us
    ppermute x2, waiting for transfers between devices, shards(): lax.ppermute(each, 'dp', ring(replicas, step))  14.2 us
    all_to_all x1, starting transfers between devices, shards(): lax.all_to_all(right_root[0, 0].reshape(parts, held, *right_root.shape[3:...  9.09 us
    ppermute x2, starting transfers between devices, shards(): lax.ppermute(each, 'dp', ring(replicas, step))  7.86 us
  transfers between devices with their start and end apart: 4, of which 3 were waited for; matrix products, arithmetic and copies ran while one was open for 3% of the time, Pallas kernels for 1%

profile of v5, /device:TPU:1, one launch (start us, length us, event | category | flops | bytes accessed | tf_op | source)
XLA Modules:
  0.0 170.7 jit_solution(2801579465483451759)
XLA Ops:
  0.0 0.0 copy-start
  0.0 1.4 copy-done
  1.4 0.1 shard_map.46
  1.6 4.8 %collective-permute-start = (bf16[256,8,128]{2,1,0:T(8,128)(2,1)S(1)}, bf16[256,8,128]{2,1,0:T(8,128)(2,1)S(1)}, u32[]{:S(2)}, u32[]{:S(2)}) collective-permute-start(bf16[256,8,128]{2,1,0:T(8,128)(2,1)S(1)} %get-tuple-element.11), channel_id=1, source_target_pairs={{0,256},{256,512},{512,0},{1,257},{257,513},{513,1},{2,258},{258,5... | collective-permute-start | bytes 1572872 | tf_op jit(solution)/shard_map/ppermute | solution.py:112
  6.4 8.4 %collective-permute-done.rest_1_ = bf16[256,8,128]{2,1,0:T(8,128)(2,1)S(1)} collective-permute-done((bf16[256,8,128]{2,1,0:T(8,128)(2,1)S(1)}, bf16[256,8,128]{2,1,0:T(8,128)(2,1)S(1)}, u32[]{:S(2)}, u32[]{:S(2)}) %collective-permute-start) | collective-permute-done | bytes 524320 | tf_op jit(solution)/shard_map/ppermute | solution.py:112
  14.8 9.1 %all-to-all-start.1 = ((bf16[4,2,512,128]{3,2,1,0:T(8,128)(2,1)}), bf16[4,2,512,128]{3,2,1,0:T(8,128)(2,1)S(1)}, u32[]{:S(2)}, u32[]{:S(2)}) async-start(bf16[4,2,512,128]{3,2,1,0:T(8,128)(2,1)} %bitcast.34), calls=%async_computation.1 | async-start | bytes 2097152 | tf_op jit(solution)/shard_map/all_to_all | solution.py:115
  23.8 3.0 %collective-permute-start.1 = (bf16[256,8,128]{2,1,0:T(8,128)(2,1)S(1)}, bf16[256,8,128]{2,1,0:T(8,128)(2,1)S(1)}, u32[]{:S(2)}, u32[]{:S(2)}) collective-permute-start(bf16[256,8,128]{2,1,0:T(8,128)(2,1)S(1)} %get-tuple-element.13), channel_id=1, source_target_pairs={{0,512},{256,0},{512,256},{1,513},{257,1},{513,257},{2,514},{258,2... | collective-permute-start | bytes 1572872 | tf_op jit(solution)/shard_map/ppermute | solution.py:112
  26.9 0.7 fusion.3
  27.6 0.6 reduce-window.6
  28.2 0.2 slice_reduce_fusion
  28.4 0.8 fusion.2
  29.2 0.7 multiply_add_fusion.target_ref.place_ref
  29.9 5.9 %collective-permute-done.1.rest_2_ = bf16[256,8,128]{2,1,0:T(8,128)(2,1)S(1)} collective-permute-done((bf16[256,8,128]{2,1,0:T(8,128)(2,1)S(1)}, bf16[256,8,128]{2,1,0:T(8,128)(2,1)S(1)}, u32[]{:S(2)}, u32[]{:S(2)}) %collective-permute-start.1) | collective-permute-done | bytes 524320 | tf_op jit(solution)/shard_map/ppermute | solution.py:112
  35.8 2.0 %shard_map.47 = bf16[512,8,128]{2,1,0:T(8,128)(2,1)} custom-call(s32[256]{0:T(256)S(1)} %multiply_add_fusion.target_ref.place_ref, bf16[256,8,128]{2,1,0:T(8,128)(2,1)S(1)} %get-tuple-element.10.rest_0_, bf16[256,8,128]{2,1,0:T(8,128)(2,1)S(1)} %collective-permute-done.rest_1_, bf16[256,8,128]{2,1,0:T(8,128)(2,1)S(1)} %collective-permute-done.1.rest_2_), custom_call_target="tpu_custom_call" | custom-call | tf_op jit(solution)/shard_map/pallas_call | solution.py:129
  37.8 0.0 all-to-all-done.1.right_ref
  37.8 29.0 %all-to-all-start = ((bf16[256,16,128]{2,1,0:T(8,128)(2,1)}), bf16[256,16,128]{2,1,0:T(8,128)(2,1)S(1)}, u32[]{:S(2)}, u32[]{:S(2)}) async-start(bf16[256,16,128]{2,1,0:T(8,128)(2,1)} %bitcast.4), calls=%async_computation | async-start | bytes 2097152 | tf_op jit(solution)/shard_map/all_to_all | solution.py:136
  66.8 1.3 dynamic-slice_bitcast_fusion.left_ref
  68.1 44.4 %all-to-all-done = bf16[256,16,128]{2,1,0:T(8,128)(2,1)S(1)} async-done(((bf16[256,16,128]{2,1,0:T(8,128)(2,1)}), bf16[256,16,128]{2,1,0:T(8,128)(2,1)S(1)}, u32[]{:S(2)}, u32[]{:S(2)}) %all-to-all-start) | async-done | bytes 1048608 | tf_op jit(solution)/shard_map/all_to_all | solution.py:136
  112.5 1.8 %shard_map.48 = bf16[64,4,16,128]{3,2,1,0:T(8,128)(2,1)S(1)} custom-call(bf16[64,4,16,128]{3,2,1,0:T(8,128)(2,1)S(1)} %bitcast.31, bf16[2,512,512]{2,1,0:T(8,128)(2,1)S(1)} %dynamic-slice_bitcast_fusion.left_ref, bf16[4,2,512,128]{3,2,1,0:T(8,128)(2,1)S(1)} %all-to-all-done.1.right_ref), custom_call_target="tpu_custom_call" | custom-call | tf_op jit(solution)/shard_map/pallas_call | solution.py:138
  114.3 54.6 %all_to_all.15 = bf16[256,16,128]{2,1,0:T(8,128)(2,1)S(1)} all-to-all(bf16[256,16,128]{2,1,0:T(8,128)(2,1)S(1)} %bitcast.32), channel_id=1, replica_groups=mesh['dp'=3,'mp'=64,'inner'=4] {'mp','inner'}, dimensions={0} | all-to-all | bytes 2097152 | tf_op jit(solution)/shard_map/all_to_all | solution.py:145
  169.0 1.7 shard_map.49
  (2 shorter events, 0.0 us)
Async XLA Ops:
  0.0 1.4 copy-start
  1.6 13.2 %collective-permute-start = (bf16[256,8,128]{2,1,0:T(8,128)(2,1)S(1)}, bf16[256,8,128]{2,1,0:T(8,128)(2,1)S(1)}, u32[]{:S(2)}, u32[]{:S(2)}) collective-permute-start(bf16[256,8,128]{2,1,0:T(8,128)(2,1)S(1)} %get-tuple-element.11), channel_id=1, source_target_pairs={{0,256},{256,512},{512,0},{1,257},{257,513},{513,1},{2,258},{258,5... | collective-permute-start | bytes 1572872 | tf_op jit(solution)/shard_map/ppermute | solution.py:112
  14.8 23.0 %all-to-all-start.1 = ((bf16[4,2,512,128]{3,2,1,0:T(8,128)(2,1)}), bf16[4,2,512,128]{3,2,1,0:T(8,128)(2,1)S(1)}, u32[]{:S(2)}, u32[]{:S(2)}) async-start(bf16[4,2,512,128]{3,2,1,0:T(8,128)(2,1)} %bitcast.34), calls=%async_computation.1 | async-start | bytes 2097152 | tf_op jit(solution)/shard_map/all_to_all | solution.py:115
  23.8 11.9 %collective-permute-start.1 = (bf16[256,8,128]{2,1,0:T(8,128)(2,1)S(1)}, bf16[256,8,128]{2,1,0:T(8,128)(2,1)S(1)}, u32[]{:S(2)}, u32[]{:S(2)}) collective-permute-start(bf16[256,8,128]{2,1,0:T(8,128)(2,1)S(1)} %get-tuple-element.13), channel_id=1, source_target_pairs={{0,512},{256,0},{512,256},{1,513},{257,1},{513,257},{2,514},{258,2... | collective-permute-start | bytes 1572872 | tf_op jit(solution)/shard_map/ppermute | solution.py:112
  37.8 74.7 %all-to-all-start = ((bf16[256,16,128]{2,1,0:T(8,128)(2,1)}), bf16[256,16,128]{2,1,0:T(8,128)(2,1)S(1)}, u32[]{:S(2)}, u32[]{:S(2)}) async-start(bf16[256,16,128]{2,1,0:T(8,128)(2,1)} %bitcast.4), calls=%async_computation | async-start | bytes 2097152 | tf_op jit(solution)/shard_map/all_to_all | solution.py:136
